TPU v7x, 32 devices: a whole 2x2x4 slice. The times are simulated.
32 devices in a mesh: brow: 8 (over z, core), bcol: 4 (over y, x).
Axes of the slice: x: 2, y: 2, z: 4, core: 2. Of those that a mesh axis runs over, the one named last changes fastest.
Arguments:
- right_side: float32 [16384, 64], P(('brow', 'bcol')), may hold values from -36 to 36
- tiles: bfloat16 [64, 1, 512, 512], P(('brow', 'bcol')), may hold values from -0.03125 to 0.03125
- row_blocks: int32 [64], P(('brow', 'bcol')), may hold values from 0 to 31, as said below
- col_blocks: int32 [64, 1], P(('brow', 'bcol')), may hold values from 0 to 31, as said below
Outputs:
- solution: float32 [16384, 64], P(('brow', 'bcol'))
- residual: float32 [16384, 64], P(('brow', 'bcol'))
Inputs may be any that keep to these rules, and one draw needn't show every extreme that they name: `row_blocks`: the 2 row blocks of one device lie in different groups, the group of block b being b % 4. `col_blocks`: the tile columns of the device at bcol index j are blocks c with c % 4 == j, different within one row slot.
All inputs are finite; a program needn't handle non-finite values.
Results may differ from a plain program's by a relative error of at most 0.0061.
Values may be sent and summed in bfloat16 or wider, within the bound.
A program may use at most 128 MiB of HBM per device.

v0:
```python
import jax
import jax.numpy as jnp
from jax import lax
from jax.sharding import PartitionSpec as P

ITERS = 3
highest = lax.Precision.HIGHEST


def solve_spd(matrix, rhs):
    factor = jnp.linalg.cholesky(matrix)
    return jax.scipy.linalg.cho_solve((factor, True), rhs)


def gram_of(left, right):
    return jnp.dot(left.T, right, precision=highest)


def right_mult(vectors, coeffs):
    return jnp.einsum("...k,kl->...l", vectors, coeffs, precision=highest)


def shards(right_side, tiles, row_blocks, col_blocks):
    groups = lax.axis_size("bcol")
    gblocks = lax.axis_size("brow")
    tile, width = right_side.shape
    slots, per_row = col_blocks.shape
    flat = tile * width
    slot_group = row_blocks % groups
    slot_place = row_blocks // groups
    col_place = col_blocks // groups
    group_ids = jnp.arange(groups, dtype=jnp.int32)
    block_ids = jnp.arange(gblocks, dtype=jnp.int32)
    matches = slot_group[:, None] == group_ids[None, :]
    wanted = jnp.sum(jnp.where(matches, slot_place[:, None], 0), axis=0)
    active = jnp.any(matches, axis=0).astype(jnp.int32)
    asked = lax.all_to_all(
        jnp.stack([wanted, active], axis=1), "bcol", split_axis=0, concat_axis=0, tiled=True
    )
    send_pick = ((asked[:, 0:1] == block_ids[None, :]) & (asked[:, 1:2] == 1)).astype(jnp.float32)
    slot_pick = matches.astype(jnp.float32)
    col_pick = (col_place.reshape(-1)[:, None] == block_ids[None, :]).astype(jnp.float32)
    own_index = lax.axis_index("brow")
    field = lax.all_gather(right_side[None], "brow", axis=0, tiled=True)

    def own(vectors):
        return lax.dynamic_index_in_dim(vectors, own_index, 0, keepdims=False)

    solution = jnp.zeros_like(field)
    residual = field
    direction = field
    rr_now = lax.psum(gram_of(own(residual), own(residual)), ("brow", "bcol"))
    for step in range(ITERS):
        stacked = direction.astype(jnp.bfloat16).reshape(gblocks, flat)
        outgoing = jnp.dot(
            send_pick.astype(jnp.bfloat16), stacked, preferred_element_type=jnp.float32
        ).astype(jnp.bfloat16)
        arrived = lax.all_to_all(outgoing, "bcol", split_axis=0, concat_axis=0, tiled=True)
        row_dir = jnp.dot(
            slot_pick.astype(jnp.bfloat16), arrived, preferred_element_type=jnp.float32
        )
        row_dir = row_dir.astype(jnp.bfloat16).reshape(slots, tile, width)
        col_dir = jnp.dot(
            col_pick.astype(jnp.bfloat16), stacked, preferred_element_type=jnp.float32
        )
        col_dir = col_dir.astype(jnp.bfloat16).reshape(slots, per_row, tile, width)
        turned = jnp.einsum("scab,sak->scbk", tiles, row_dir, preferred_element_type=jnp.float32)
        direct = jnp.einsum("scab,scbk->sak", tiles, col_dir, preferred_element_type=jnp.float32)
        local = jnp.dot(col_pick.T, turned.reshape(slots * per_row, flat), precision=highest)
        pushing = jnp.dot(slot_pick.T, direct.reshape(slots, flat), precision=highest)
        returned = lax.all_to_all(pushing, "bcol", split_axis=0, concat_axis=0, tiled=True)
        local = local + jnp.dot(send_pick.T, returned, precision=highest)
        summed = lax.psum(local.reshape(gblocks, tile, width), "brow")
        image = 3.0 * direction + summed
        curve = lax.psum(gram_of(own(direction), own(image)), ("brow", "bcol"))
        alpha = solve_spd(curve, rr_now)
        solution = solution + right_mult(direction, alpha)
        residual = residual - right_mult(image, alpha)
        if step + 1 < ITERS:
            fresh = lax.psum(gram_of(own(residual), own(residual)), ("brow", "bcol"))
            beta = solve_spd(rr_now, fresh)
            direction = residual + right_mult(direction, beta)
            rr_now = fresh
    return (own(solution), own(residual))


def solution(mesh):
    placed = (
        P(("brow", "bcol"), None),
        P(("brow", "bcol"), None, None, None),
        P(("brow", "bcol")),
        P(("brow", "bcol"), None),
    )
    return jax.shard_map(
        shards,
        mesh=mesh,
        in_specs=placed,
        out_specs=(P(("brow", "bcol"), None), P(("brow", "bcol"), None)),
        check_vma=False,
    )
```

profile of v0, /device:TPU:0, one launch (start us, length us, event | category | flops | bytes accessed | tf_op | source)
XLA Modules:
  0.0 628.7 jit_solution(16731248828745427380)
XLA Ops:
  9.4 5.2 all-to-all-start
  15.3 3.9 all-to-all-done
  19.4 15.1 %all-gather.3.cloned.1.call-done = f32[4096,64]{0,1:T(8,128)} async-done(((f32[512,64]{0,1:T(8,128)}), f32[4096,64]{0,1:T(8,128)}) %all-gather.3.cloned.1.call-update) | async-done | bytes 1048592 | tf_op jit(solution)/shard_map/all_gather | solution.py:44
  34.5 1.8 copy.235
  37.9 2.0 reshape.113
  43.1 3.6 all-to-all-start.1
  50.0 2.5 all-to-all-done.1
  52.5 4.1 all-to-all-start.2
  58.4 1.8 fusion.87
  60.2 3.8 all-to-all-done.2
  64.0 2.4 convolution_add_fusion.2
  66.4 2.2 reshape.119
  68.6 3.2 copy.173
  72.3 57.7 %all-reduce.5.cloned.1.call-done = f32[8,512,64]{1,2,0:T(8,128)} async-done(((f32[8,512,64]{1,2,0:T(8,128)}), f32[8,512,64]{1,2,0:T(8,128)}) %all-reduce.5.cloned.1.call-update) | async-done | bytes 1048592 | tf_op jit(solution)/shard_map/psum | solution.py:73
  131.8 40.0 %all-reduce = (f32[64,64]{0,1:T(8,128)S(1)}, f32[64,64]{0,1:T(8,128)S(1)}) all-reduce(f32[64,64]{0,1:T(8,128)S(1)} %fusion.29, f32[64,64]{0,1:T(8,128)S(1)} %fusion.31), channel_id=1, replica_groups=mesh['brow'=8,'bcol'=4] {'brow','bcol'}, use_global_device_ids=true, to_apply=%region_6.8 | all-reduce | flops 8192 | bytes 65536 | tf_op jit(solution)/shard_map/psum | solution.py:52
  171.8 5.8 cholesky.89
  179.0 4.9 custom-call.11
  187.1 40.0 %psum.66 = f32[64,64]{0,1:T(8,128)S(1)} all-reduce(f32[64,64]{0,1:T(8,128)S(1)} %fusion.41), channel_id=1, replica_groups=mesh['brow'=8,'bcol'=4] {'brow','bcol'}, use_global_device_ids=true, to_apply=%region_7.10 | all-reduce | flops 4096 | bytes 32768 | tf_op jit(solution)/shard_map/psum | solution.py:80
  227.1 5.8 cholesky.100
  234.3 4.9 custom-call.12
  239.7 3.1 fusion.102
  242.8 2.4 copy.185
  245.2 2.9 reshape.120
  248.0 2.0 convolution_convert_fusion.5
  250.1 2.0 fusion.1
  252.1 1.9 reduce.5
  255.0 4.7 all-to-all-start.3
  259.7 1.8 reshape.123
  261.5 2.1 convolution_bitcast_fusion.7
  263.7 2.0 copy.190
  265.6 2.0 reshape.124
  270.7 4.2 all-to-all-start.4
  281.9 1.8 fusion.86
  283.7 3.4 convolution_add_fusion.1
  287.1 3.4 reshape.125
  290.5 3.2 copy.192
  293.7 5.8 cholesky.122
  300.9 4.9 custom-call.14
  305.8 46.6 %all-reduce.7.cloned.1.call-done = f32[8,512,64]{1,2,0:T(8,128)} async-done(((f32[8,512,64]{1,2,0:T(8,128)}), f32[8,512,64]{1,2,0:T(8,128)}) %all-reduce.7.cloned.1.call-update) | async-done | bytes 1048592 | tf_op jit(solution)/shard_map/psum | solution.py:73
  355.1 39.8 %psum.68 = f32[64,64]{0,1:T(8,128)S(1)} all-reduce(f32[64,64]{0,1:T(8,128)S(1)} %fusion.38), channel_id=1, replica_groups=mesh['brow'=8,'bcol'=4] {'brow','bcol'}, use_global_device_ids=true, to_apply=%region_9.12 | all-reduce | flops 4096 | bytes 32768 | tf_op jit(solution)/shard_map/psum | solution.py:75
  395.0 5.8 cholesky.111
  402.2 4.9 custom-call.13
  408.2 2.7 convolution_subtract_fusion
  412.2 40.0 %psum.69 = f32[64,64]{1,0:T(8,128)S(1)} all-reduce(f32[64,64]{1,0:T(8,128)S(1)} %fusion.36), channel_id=1, replica_groups=mesh['brow'=8,'bcol'=4] {'brow','bcol'}, use_global_device_ids=true, to_apply=%region_10.13 | all-reduce | flops 4096 | bytes 32768 | tf_op jit(solution)/shard_map/psum | solution.py:80
  452.7 3.6 fusion.103
  456.2 2.4 copy.199
  458.6 2.9 reshape.126
  462.9 2.0 fusion.2
  464.9 1.9 reduce.6
  467.8 4.5 all-to-all-start.5
  473.2 2.1 convolution_bitcast_fusion.5
  475.3 1.9 copy.204
  477.3 2.0 reshape.130
  482.4 4.2 all-to-all-start.6
  495.5 3.3 convolution_add_fusion
  498.9 3.4 reshape.131
  502.3 3.2 copy.206
  505.5 2.0 convolution_bitcast_fusion.4
  507.5 2.1 fusion.104
  509.6 54.4 %all-reduce.9.cloned.1.call-done = f32[8,512,64]{1,2,0:T(8,128)} async-done(((f32[8,512,64]{1,2,0:T(8,128)}), f32[8,512,64]{1,2,0:T(8,128)}) %all-reduce.9.cloned.1.call-update) | async-done | bytes 1048592 | tf_op jit(solution)/shard_map/psum | solution.py:73
  565.9 39.4 %psum.71 = f32[64,64]{0,1:T(8,128)S(1)} all-reduce(f32[64,64]{0,1:T(8,128)S(1)} %fusion.33), channel_id=1, replica_groups=mesh['brow'=8,'bcol'=4] {'brow','bcol'}, use_global_device_ids=true, to_apply=%region_12.15 | all-reduce | flops 4096 | bytes 32768 | tf_op jit(solution)/shard_map/psum | solution.py:75
  605.4 5.8 cholesky.133
  612.6 4.9 custom-call.15
  620.2 1.8 fusion.27
  (137 shorter events, 62.0 us)
Async XLA Ops:
  7.2 39.7 %copy-start = (bf16[2,1,512,512]{3,2,1,0:T(8,128)(2,1)S(1)}, bf16[2,1,512,512]{3,2,1,0:T(8,128)(2,1)}, u32[]{:S(2)}) copy-start(bf16[2,1,512,512]{3,2,1,0:T(8,128)(2,1)} %param.8) | copy-start | bytes 3145732
  7.2 27.3 %all-gather.3.cloned.1.call-start = ((), (), s32[]{:S(2)}) async-start(), calls=%async_computation.10 | async-start | bytes 1179648 | tf_op jit(solution)/shard_map/all_gather | solution.py:44
  9.4 9.7 %all-to-all-start = ((s32[4,1,2]{2,1,0:T(1,128)}), s32[4,1,2]{2,1,0:T(1,128)S(1)}, u32[]{:S(2)}, u32[]{:S(2)}) async-start(s32[4,1,2]{2,1,0:T(1,128)} %copy.164), calls=%async_computation | async-start | bytes 4096 | tf_op jit(solution)/shard_map/all_to_all | solution.py:37
  43.1 9.4 %all-to-all-start.1 = ((bf16[4,2,16384]{2,1,0:T(2,128)(2,1)}), bf16[4,2,16384]{2,1,0:T(2,128)(2,1)S(1)}, u32[]{:S(2)}, u32[]{:S(2)}) async-start(bf16[4,2,16384]{2,1,0:T(2,128)(2,1)} %reshape.142), calls=%async_computation.1 | async-start | bytes 524288 | tf_op jit(solution)/shard_map/all_to_all | solution.py:58
  52.5 11.6 %all-to-all-start.2 = ((f32[4,1,32768]{2,1,0:T(1,128)}), f32[4,1,32768]{2,1,0:T(1,128)}, u32[]{:S(2)}, u32[]{:S(2)}) async-start(f32[4,1,32768]{2,1,0:T(1,128)} %copy.172), calls=%async_computation.2 | async-start | bytes 1048576 | tf_op jit(solution)/shard_map/all_to_all | solution.py:71
  56.6 73.3 %all-reduce.5.cloned.1.call-start = ((), (), s32[]{:S(2)}) async-start(), calls=%async_computation.7 | async-start | bytes 2097152 | tf_op jit(solution)/shard_map/psum | solution.py:73
  68.6 61.3 %copy-start.1 = (f32[4096,64]{0,1:T(8,128)S(1)}, f32[4096,64]{0,1:T(8,128)}, u32[]{:S(2)}) copy-start(f32[4096,64]{0,1:T(8,128)} %all-gather.3.cloned.1.call-done) | copy-start | bytes 3145732
  129.9 54.6 %copy-start.6 = (f32[8,512,64]{1,2,0:T(8,128)S(1)}, f32[8,512,64]{1,2,0:T(8,128)}, u32[]{:S(2)}) copy-start(f32[8,512,64]{1,2,0:T(8,128)} %all-reduce.5.cloned.1.call-done) | copy-start | bytes 3145732
  184.5 1.3 copy-start.7
  185.8 1.0 copy-start.2
  255.0 15.7 %all-to-all-start.3 = ((bf16[4,2,16384]{2,1,0:T(2,128)(2,1)}), bf16[4,2,16384]{2,1,0:T(2,128)(2,1)S(1)}, u32[]{:S(2)}, u32[]{:S(2)}) async-start(bf16[4,2,16384]{2,1,0:T(2,128)(2,1)} %reshape.144), calls=%async_computation.3 | async-start | bytes 524288 | tf_op jit(solution)/shard_map/all_to_all | solution.py:58
  270.7 13.0 %all-to-all-start.4 = ((f32[4,1,32768]{2,1,0:T(1,128)}), f32[4,1,32768]{2,1,0:T(1,128)}, u32[]{:S(2)}, u32[]{:S(2)}) async-start(f32[4,1,32768]{2,1,0:T(1,128)} %copy.191), calls=%async_computation.4 | async-start | bytes 1048576 | tf_op jit(solution)/shard_map/all_to_all | solution.py:71
  274.9 77.4 %all-reduce.7.cloned.1.call-start = ((), (), s32[]{:S(2)}) async-start(), calls=%async_computation.8 | async-start | bytes 2097152 | tf_op jit(solution)/shard_map/psum | solution.py:73
  353.8 1.0 copy-start.5
  407.6 0.6 copy-start.9
  410.9 1.0 copy-start.4
  452.2 6.4 %copy-start.11 = (f32[64,64]{1,0:T(8,128)}, f32[64,64]{1,0:T(8,128)S(1)}, u32[]{:S(2)}) copy-start(f32[64,64]{1,0:T(8,128)S(1)} %psum.69) | copy-start | bytes 49156
  467.8 14.5 %all-to-all-start.5 = ((bf16[4,2,16384]{2,1,0:T(2,128)(2,1)}), bf16[4,2,16384]{2,1,0:T(2,128)(2,1)S(1)}, u32[]{:S(2)}, u32[]{:S(2)}) async-start(bf16[4,2,16384]{2,1,0:T(2,128)(2,1)} %reshape.146), calls=%async_computation.5 | async-start | bytes 524288 | tf_op jit(solution)/shard_map/all_to_all | solution.py:58
  482.4 13.2 %all-to-all-start.6 = ((f32[4,1,32768]{2,1,0:T(1,128)}), f32[4,1,32768]{2,1,0:T(1,128)}, u32[]{:S(2)}, u32[]{:S(2)}) async-start(f32[4,1,32768]{2,1,0:T(1,128)} %copy.205), calls=%async_computation.6 | async-start | bytes 1048576 | tf_op jit(solution)/shard_map/all_to_all | solution.py:71
  486.6 77.5 %all-reduce.9.cloned.1.call-start = ((), (), s32[]{:S(2)}) async-start(), calls=%async_computation.9 | async-start | bytes 2097152 | tf_op jit(solution)/shard_map/psum | solution.py:73
  502.3 3.2 copy-start.8
  505.4 2.1 copy-start.10
  507.5 56.6 %copy-start.3 = (f32[8,512,64]{1,2,0:T(8,128)S(1)}, f32[8,512,64]{1,2,0:T(8,128)}, u32[]{:S(2)}) copy-start(f32[8,512,64]{1,2,0:T(8,128)} %get-tuple-element.11) | copy-start | bytes 3145732
  509.6 107.9 %copy-start.12 = (f32[64,64]{1,0:T(8,128)S(1)}, f32[64,64]{1,0:T(8,128)}, u32[]{:S(2)}) copy-start(f32[64,64]{1,0:T(8,128)} %copy-done.11) | copy-start | bytes 49156
Sparse Core Ops, SparseCore 0:
  9.6 24.7 all-gather.2
  72.0 57.8 all-reduce.4
  293.8 58.5 all-reduce.6
  505.6 58.4 all-reduce.8
where the time goes:
time: 639 us; the launch traced here: 629 us
  blocking collectives  199 us (31%)
  waiting for transfers between devices  185 us (29%)
  other arithmetic  73 us (11%)
  local copies, waits for them, and re-layouts  67.7 us (11%)
  matrix products  58.6 us (9%)
  starting transfers between devices  30.7 us (5%)
  between operations  14.6 us (2%)
    psum x3, waiting for transfers between devices, shards(): summed = lax.psum(local.reshape(gblocks, tile, width), 'brow')  159 us
    psum x2, blocking collectives, shards(): fresh = lax.psum(gram_of(own(residual), own(residual)), ('brow', 'bcol'))  80 us
    psum x2, blocking collectives, shards(): curve = lax.psum(gram_of(own(direction), own(image)), ('brow', 'bcol'))  79.3 us
    psum x1, blocking collectives, shards(): rr_now = lax.psum(gram_of(own(residual), own(residual)), ('brow', 'bcol'))  40 us
    another operation x15, other arithmetic, solve_spd(): factor = jnp.linalg.cholesky(matrix)  32.6 us
    another operation x10, other arithmetic, solve_spd(): return jax.scipy.linalg.cho_solve((factor, True), rhs)  27.7 us
    reshape x6, local copies, waits for them, and re-layouts, shards(): summed = lax.psum(local.reshape(gblocks, tile, width), 'brow')  18.6 us
    dot_general x8, matrix products, right_mult(): return jnp.einsum('...k,kl->...l', vectors, coeffs, precision=highest)  17 us
  transfers between devices with their start and end apart: 11, of which 7 were waited for; matrix products, arithmetic and copies ran while one was open for 10% of the time, Pallas kernels for 0%

commit v1 on v0

--- a/solution.py
+++ b/solution.py
@@ -77,7 +77,9 @@
         solution = solution + right_mult(direction, alpha)
         residual = residual - right_mult(image, alpha)
         if step + 1 < ITERS:
-            fresh = lax.psum(gram_of(own(residual), own(residual)), ("brow", "bcol"))
+            own_2 = gram_of(own(residual), own(residual))
+            parts = lax.all_gather(own_2, ("brow", "bcol"), axis=0, tiled=False)
+            fresh = parts.sum(axis=0)
             beta = solve_spd(rr_now, fresh)
             direction = residual + right_mult(direction, beta)
             rr_now = fresh

time: 639 us -> 716 us (1.12)
  blocking collectives: 199 us -> 268 us
  starting transfers between devices: 30.7 us -> 40.2 us
    all_gather x0 -> x2, blocking collectives: none -> 149 us  [shards(): parts = lax.all_gather(own_2, ('brow', 'bcol'), axis=0, tiled=False)]
    psum x2 -> x0, blocking collectives: 80 us -> none  [shards(): fresh = lax.psum(gram_of(own(residual), own(residual)), ('brow', 'bcol'))]
    psum x3, starting transfers between devices: 0.21 us -> 12.1 us  [shards(): summed = lax.psum(local.reshape(gblocks, tile, width), 'brow')]
  transfers between devices with their start and end apart: 11 -> 11, of which waited for: 7 -> 7; matrix products, arithmetic and copies ran while one was open for 10% -> 9% of each run, Pallas kernels for 0% -> 0%
where the time goes in v1:
time: 716 us; the launch traced here: 705 us
  blocking collectives  268 us (37%)
  waiting for transfers between devices  183 us (26%)
  other arithmetic  74.4 us (10%)
  local copies, waits for them, and re-layouts  67.1 us (9%)
  matrix products  58.5 us (8%)
  starting transfers between devices  40.2 us (6%)
  between operations  14.8 us (2%)
    psum x3, waiting for transfers between devices, shards(): summed = lax.psum(local.reshape(gblocks, tile, width), 'brow')  157 us
    all_gather x2, blocking collectives, shards(): parts = lax.all_gather(own_2, ('brow', 'bcol'), axis=0, tiled=False)  149 us
    psum x2, blocking collectives, shards(): curve = lax.psum(gram_of(own(direction), own(image)), ('brow', 'bcol'))  78.9 us
    psum x1, blocking collectives, shards(): rr_now = lax.psum(gram_of(own(residual), own(residual)), ('brow', 'bcol'))  40 us
    another operation x15, other arithmetic, solve_spd(): factor = jnp.linalg.cholesky(matrix)  32.6 us
    another operation x10, other arithmetic, solve_spd(): return jax.scipy.linalg.cho_solve((factor, True), rhs)  27.7 us
    reshape x6, local copies, waits for them, and re-layouts, shards(): summed = lax.psum(local.reshape(gblocks, tile, width), 'brow')  18.6 us
    dot_general x8, matrix products, right_mult(): return jnp.einsum('...k,kl->...l', vectors, coeffs, precision=highest)  17 us
  transfers between devices with their start and end apart: 11, of which 7 were waited for; matrix products, arithmetic and copies ran while one was open for 9% of the time, Pallas kernels for 0%

profile of v1, /device:TPU:0, one launch (start us, length us, event | category | flops | bytes accessed | tf_op | source)
XLA Modules:
  0.0 705.3 jit_solution(593504096018416025)
XLA Ops:
  9.4 5.2 all-to-all-start
  15.3 3.9 all-to-all-done
  19.4 15.1 %all-gather.5.cloned.1.call-done = f32[4096,64]{0,1:T(8,128)} async-done(((f32[512,64]{0,1:T(8,128)}), f32[4096,64]{0,1:T(8,128)}) %all-gather.5.cloned.1.call-update) | async-done | bytes 1048592 | tf_op jit(solution)/shard_map/all_gather | solution.py:44
  34.5 1.8 copy.229
  37.9 2.0 reshape.113
  43.1 3.6 all-to-all-start.1
  50.0 2.5 all-to-all-done.1
  52.5 4.1 all-to-all-start.2
  58.4 1.8 fusion.87
  60.2 3.8 all-to-all-done.2
  64.0 2.4 convolution_add_fusion.2
  66.4 2.2 reshape.119
  68.6 3.2 copy.169
  72.3 57.7 %all-reduce.5.cloned.1.call-done = f32[8,512,64]{1,2,0:T(8,128)} async-done(((f32[8,512,64]{1,2,0:T(8,128)}), f32[8,512,64]{1,2,0:T(8,128)}) %all-reduce.5.cloned.1.call-update) | async-done | bytes 1048592 | tf_op jit(solution)/shard_map/psum | solution.py:73
  131.8 40.0 %all-reduce = (f32[64,64]{0,1:T(8,128)S(1)}, f32[64,64]{0,1:T(8,128)S(1)}) all-reduce(f32[64,64]{0,1:T(8,128)S(1)} %fusion.29, f32[64,64]{0,1:T(8,128)S(1)} %fusion.31), channel_id=1, replica_groups=mesh['brow'=8,'bcol'=4] {'brow','bcol'}, use_global_device_ids=true, to_apply=%region_6.8 | all-reduce | flops 8192 | bytes 65536 | tf_op jit(solution)/shard_map/psum | solution.py:52
  171.9 5.8 cholesky.89
  179.1 4.9 custom-call.11
  187.2 5.8 cholesky.100
  194.4 4.9 custom-call.12
  199.3 72.1 %all-gather.1 = f32[2048,64]{1,0:T(8,128)S(1)} all-gather(f32[64,64]{1,0:T(8,128)S(1)} %fusion.41), channel_id=3, replica_groups=mesh['brow'=8,'bcol'=4] {'brow','bcol'}, dimensions={0}, use_global_device_ids=true | all-gather | bytes 540672 | tf_op jit(solution)/shard_map/all_gather | solution.py:81
  271.9 3.1 fusion.102
  275.0 2.4 copy.180
  277.4 2.9 reshape.120
  280.2 2.0 convolution_convert_fusion.5
  282.3 2.0 fusion.1
  284.3 1.9 reduce.5
  287.2 3.4 all-to-all-start.3
  290.6 1.8 reshape.123
  292.4 2.1 convolution_bitcast_fusion.7
  294.6 2.0 copy.185
  296.6 2.0 reshape.124
  301.6 4.2 all-to-all-start.4
  305.8 11.8 %all-reduce.7.cloned.1.call-start = ((), (), s32[]{:S(2)}) async-start(), calls=%async_computation.8 | async-start | bytes 2097152 | tf_op jit(solution)/shard_map/psum | solution.py:73
  326.4 3.4 convolution_add_fusion.1
  329.8 3.4 reshape.125
  333.2 3.2 copy.187
  336.4 5.8 cholesky.122
  343.6 4.9 custom-call.14
  348.5 45.5 %all-reduce.7.cloned.1.call-done = f32[8,512,64]{1,2,0:T(8,128)} async-done(((f32[8,512,64]{1,2,0:T(8,128)}), f32[8,512,64]{1,2,0:T(8,128)}) %all-reduce.7.cloned.1.call-update) | async-done | bytes 1048592 | tf_op jit(solution)/shard_map/psum | solution.py:73
  396.7 39.4 %psum.53 = f32[64,64]{0,1:T(8,128)S(1)} all-reduce(f32[64,64]{0,1:T(8,128)S(1)} %fusion.38), channel_id=1, replica_groups=mesh['brow'=8,'bcol'=4] {'brow','bcol'}, use_global_device_ids=true, to_apply=%region_9.12 | all-reduce | flops 4096 | bytes 32768 | tf_op jit(solution)/shard_map/psum | solution.py:75
  436.2 5.8 cholesky.111
  443.4 4.9 custom-call.13
  448.8 2.7 convolution_subtract_fusion
  452.8 76.6 %all-gather.2 = f32[2048,64]{1,0:T(8,128)} all-gather(f32[64,64]{1,0:T(8,128)S(1)} %fusion.36), channel_id=4, replica_groups=mesh['brow'=8,'bcol'=4] {'brow','bcol'}, dimensions={0}, use_global_device_ids=true | all-gather | bytes 540672 | tf_op jit(solution)/shard_map/all_gather | solution.py:81
  531.2 3.6 fusion.103
  534.8 2.4 copy.194
  537.1 2.9 reshape.126
  541.4 2.0 fusion.2
  543.4 1.9 reduce.6
  546.3 3.4 all-to-all-start.5
  550.7 2.1 convolution_bitcast_fusion.5
  552.8 1.9 copy.199
  554.7 2.0 reshape.130
  559.8 4.2 all-to-all-start.6
  573.0 3.3 convolution_add_fusion
  576.3 3.4 reshape.131
  579.7 3.2 copy.201
  582.9 2.0 convolution_bitcast_fusion.4
  585.0 2.1 fusion.104
  587.1 53.4 %all-reduce.9.cloned.1.call-done = f32[8,512,64]{1,2,0:T(8,128)} async-done(((f32[8,512,64]{1,2,0:T(8,128)}), f32[8,512,64]{1,2,0:T(8,128)}) %all-reduce.9.cloned.1.call-update) | async-done | bytes 1048592 | tf_op jit(solution)/shard_map/psum | solution.py:73
  642.3 39.4 %psum.55 = f32[64,64]{0,1:T(8,128)S(1)} all-reduce(f32[64,64]{0,1:T(8,128)S(1)} %fusion.33), channel_id=1, replica_groups=mesh['brow'=8,'bcol'=4] {'brow','bcol'}, use_global_device_ids=true, to_apply=%region_12.15 | all-reduce | flops 4096 | bytes 32768 | tf_op jit(solution)/shard_map/psum | solution.py:75
  681.9 5.8 cholesky.133
  689.0 4.9 custom-call.15
  696.6 1.8 fusion.27
  (139 shorter events, 64.6 us)
Async XLA Ops:
  7.2 39.7 %copy-start = (bf16[2,1,512,512]{3,2,1,0:T(8,128)(2,1)S(1)}, bf16[2,1,512,512]{3,2,1,0:T(8,128)(2,1)}, u32[]{:S(2)}) copy-start(bf16[2,1,512,512]{3,2,1,0:T(8,128)(2,1)} %param.8) | copy-start | bytes 3145732
  7.2 27.3 %all-gather.5.cloned.1.call-start = ((), (), s32[]{:S(2)}) async-start(), calls=%async_computation.10 | async-start | bytes 1179648 | tf_op jit(solution)/shard_map/all_gather | solution.py:44
  9.4 9.7 %all-to-all-start = ((s32[4,1,2]{2,1,0:T(1,128)}), s32[4,1,2]{2,1,0:T(1,128)S(1)}, u32[]{:S(2)}, u32[]{:S(2)}) async-start(s32[4,1,2]{2,1,0:T(1,128)} %copy.160), calls=%async_computation | async-start | bytes 4096 | tf_op jit(solution)/shard_map/all_to_all | solution.py:37
  43.1 9.4 %all-to-all-start.1 = ((bf16[4,2,16384]{2,1,0:T(2,128)(2,1)}), bf16[4,2,16384]{2,1,0:T(2,128)(2,1)S(1)}, u32[]{:S(2)}, u32[]{:S(2)}) async-start(bf16[4,2,16384]{2,1,0:T(2,128)(2,1)} %reshape.144), calls=%async_computation.1 | async-start | bytes 524288 | tf_op jit(solution)/shard_map/all_to_all | solution.py:58
  52.5 11.6 %all-to-all-start.2 = ((f32[4,1,32768]{2,1,0:T(1,128)}), f32[4,1,32768]{2,1,0:T(1,128)}, u32[]{:S(2)}, u32[]{:S(2)}) async-start(f32[4,1,32768]{2,1,0:T(1,128)} %copy.168), calls=%async_computation.2 | async-start | bytes 1048576 | tf_op jit(solution)/shard_map/all_to_all | solution.py:71
  56.6 73.3 %all-reduce.5.cloned.1.call-start = ((), (), s32[]{:S(2)}) async-start(), calls=%async_computation.7 | async-start | bytes 2097152 | tf_op jit(solution)/shard_map/psum | solution.py:73
  68.6 61.3 %copy-start.1 = (f32[4096,64]{0,1:T(8,128)S(1)}, f32[4096,64]{0,1:T(8,128)}, u32[]{:S(2)}) copy-start(f32[4096,64]{0,1:T(8,128)} %all-gather.5.cloned.1.call-done) | copy-start | bytes 3145732
  129.9 54.6 %copy-start.6 = (f32[8,512,64]{1,2,0:T(8,128)S(1)}, f32[8,512,64]{1,2,0:T(8,128)}, u32[]{:S(2)}) copy-start(f32[8,512,64]{1,2,0:T(8,128)} %all-reduce.5.cloned.1.call-done) | copy-start | bytes 3145732
  184.6 2.6 copy-start.7
  185.9 1.0 copy-start.2
  287.2 14.4 %all-to-all-start.3 = ((bf16[4,2,16384]{2,1,0:T(2,128)(2,1)}), bf16[4,2,16384]{2,1,0:T(2,128)(2,1)S(1)}, u32[]{:S(2)}, u32[]{:S(2)}) async-start(bf16[4,2,16384]{2,1,0:T(2,128)(2,1)} %reshape.146), calls=%async_computation.3 | async-start | bytes 524288 | tf_op jit(solution)/shard_map/all_to_all | solution.py:58
  301.6 24.8 %all-to-all-start.4 = ((f32[4,1,32768]{2,1,0:T(1,128)}), f32[4,1,32768]{2,1,0:T(1,128)}, u32[]{:S(2)}, u32[]{:S(2)}) async-start(f32[4,1,32768]{2,1,0:T(1,128)} %copy.186), calls=%async_computation.4 | async-start | bytes 1048576 | tf_op jit(solution)/shard_map/all_to_all | solution.py:71
  305.8 88.2 %all-reduce.7.cloned.1.call-start = ((), (), s32[]{:S(2)}) async-start(), calls=%async_computation.8 | async-start | bytes 2097152 | tf_op jit(solution)/shard_map/psum | solution.py:73
  395.4 1.0 copy-start.5
  448.8 80.6 %copy-start.9 = (f32[64,64,1]{0,1,2:T(8,128)}, f32[64,64,1]{0,1,2:T(8,128)S(1)}, u32[]{:S(2)}) copy-start(f32[64,64,1]{0,1,2:T(8,128)S(1)} %convolution_bitcast_fusion.13) | copy-start | bytes 49156
  451.5 1.0 copy-start.4
  530.7 6.4 copy-start.11
  546.3 13.5 %all-to-all-start.5 = ((bf16[4,2,16384]{2,1,0:T(2,128)(2,1)}), bf16[4,2,16384]{2,1,0:T(2,128)(2,1)S(1)}, u32[]{:S(2)}, u32[]{:S(2)}) async-start(bf16[4,2,16384]{2,1,0:T(2,128)(2,1)} %reshape.148), calls=%async_computation.5 | async-start | bytes 524288 | tf_op jit(solution)/shard_map/all_to_all | solution.py:58
  559.8 13.2 %all-to-all-start.6 = ((f32[4,1,32768]{2,1,0:T(1,128)}), f32[4,1,32768]{2,1,0:T(1,128)}, u32[]{:S(2)}, u32[]{:S(2)}) async-start(f32[4,1,32768]{2,1,0:T(1,128)} %copy.200), calls=%async_computation.6 | async-start | bytes 1048576 | tf_op jit(solution)/shard_map/all_to_all | solution.py:71
  564.0 76.6 %all-reduce.9.cloned.1.call-start = ((), (), s32[]{:S(2)}) async-start(), calls=%async_computation.9 | async-start | bytes 2097152 | tf_op jit(solution)/shard_map/psum | solution.py:73
  579.7 3.2 copy-start.8
  582.9 2.1 copy-start.10
  585.0 55.6 %copy-start.3 = (f32[8,512,64]{1,2,0:T(8,128)S(1)}, f32[8,512,64]{1,2,0:T(8,128)}, u32[]{:S(2)}) copy-start(f32[8,512,64]{1,2,0:T(8,128)} %get-tuple-element.11) | copy-start | bytes 3145732
  587.1 106.9 %copy-start.12 = (f32[64,64]{1,0:T(8,128)S(1)}, f32[64,64]{1,0:T(8,128)}, u32[]{:S(2)}) copy-start(f32[64,64]{1,0:T(8,128)} %copy-done.11) | copy-start | bytes 49156
Sparse Core Ops, SparseCore 0:
  9.6 24.7 all-gather.4
  72.0 57.8 all-reduce.4
  336.5 57.4 all-reduce.6
  583.0 57.4 all-reduce.8
